TPU v7x, 32 devices: a whole 2x2x4 slice. The times are simulated.
32 devices in a mesh: group: 8 (over z, x), tensor: 4 (over y, core).
Axes of the slice: x: 2, y: 2, z: 4, core: 2. Of those that a mesh axis runs over, the one named last changes fastest.
Arguments:
- tokens: bfloat16 [4096, 8192], P('group'), may hold values from -6 to 6
- norm_gain: float32 [8192], replicated, may hold values from 0.1 to 1.9
- w_key: bfloat16 [8192, 1024], P('group', 'tensor'), may hold values from -0.0625 to 0.0625
- w_value: bfloat16 [8192, 1024], P('group', 'tensor'), may hold values from -0.0625 to 0.0625
- positions: int32 [4096], P('group'), may hold values from 0 to 8191, as said below
- page_owner: int32 [256, 1], replicated, may hold values from 0 to 7; in each aligned block of 32 rows (0 to 31, 32 to 63, ...) at most 8 rows name the same one
- queries: bfloat16 [512, 8192], P('group', 'tensor'), may hold values from -100 to 100, as said below
- kv_cache: bfloat16 [512, 64, 2, 8, 128], P('group', None, None, 'tensor'), may hold values from -5 to 5
- cache_lengths: int32 [512], P('group'), may hold values from 2 to 64
Outputs:
- decoded: bfloat16 [512, 8192], P('group', 'tensor')
Inputs may be any that keep to these rules, and one draw needn't show every extreme that they name: The queries are real values of order one or a few tens. Each page's tokens have consecutive positions. `page_owner`: at most 8 of one group index's pages go to one owner.
All inputs are finite; a program needn't handle non-finite values.
Results may differ from a plain program's by a relative error of at most 0.0054.
Values may be sent and summed in bfloat16 or wider, within the bound.
A program may use at most 192 MiB of HBM per device.

v0:
```python
import math

import jax
import jax.numpy as jnp
from jax import lax
from jax.sharding import PartitionSpec as P

HD = 128
PAGE = 16
CAP = 8


def rotate(keys, positions):
    half = keys.shape[-1] // 2
    index = jnp.arange(half).astype(jnp.float32)
    inverse = jnp.exp(index * (-2.0 * math.log(500000.0) / keys.shape[-1]))
    angles = positions.astype(jnp.float32)[:, None] * inverse[None, :]
    cosine = jnp.cos(angles)[:, None, :]
    sine = jnp.sin(angles)[:, None, :]
    first = keys[..., :half]
    second = keys[..., half:]
    return jnp.concatenate([first * cosine - second * sine, second * cosine + first * sine], -1)


def attend(queries, kv_cache, placed, filled, lengths):
    count = queries.shape[0]
    heads = kv_cache.shape[3]
    span = kv_cache.shape[1]
    query_b = queries.reshape(count, heads, -1, HD)
    scale = 1.0 / math.sqrt(HD)
    near = (
        jnp.einsum(
            "rhgd,rlhd->rhgl", query_b, kv_cache[:, :, 0], preferred_element_type=jnp.float32
        )
        * scale
    )
    fresh = (
        jnp.einsum("rhgd,rphd->rhgp", query_b, placed[:, :, 0], preferred_element_type=jnp.float32)
        * scale
    )
    cache_ok = (jnp.arange(span)[None, :] < lengths[:, None])[:, None, None, :]
    page_ok = (filled > 0)[:, None, None, None]
    scores = jnp.concatenate(
        [jnp.where(cache_ok, near, -1e30), jnp.where(page_ok, fresh, -1e30)], -1
    )
    top = jnp.max(scores, -1, keepdims=True)
    weights = jnp.exp(scores - top)
    total = jnp.sum(weights, -1, keepdims=True)
    probs = (weights / total).astype(jnp.bfloat16)
    output = jnp.einsum(
        "rhgl,rlhd->rhgd", probs[..., :span], kv_cache[:, :, 1], preferred_element_type=jnp.float32
    )
    output = output + jnp.einsum(
        "rhgp,rphd->rhgd", probs[..., span:], placed[:, :, 1], preferred_element_type=jnp.float32
    )
    return output.reshape(count, -1).astype(jnp.bfloat16)


def per_device(
    tokens, norm_gain, w_key, w_value, positions, page_owner, queries, kv_cache, cache_lengths
):
    tok_count = tokens.shape[0]
    values = tokens.astype(jnp.float32)
    factor = lax.rsqrt(jnp.mean(values * values, -1, keepdims=True) + 1e-05)
    normed = (values * factor * norm_gain[None, :]).astype(jnp.bfloat16)
    full_key, full_value = (
        lax.all_gather(w_key, "group", axis=0, tiled=True),
        lax.all_gather(w_value, "group", axis=0, tiled=True),
    )
    key_sum = jnp.dot(normed, full_key, preferred_element_type=jnp.float32)
    value_sum = jnp.dot(normed, full_value, preferred_element_type=jnp.float32)
    heads = w_key.shape[1] // HD
    keys = rotate(key_sum.reshape(tok_count, heads, HD), positions).astype(jnp.bfloat16)
    vals = value_sum.astype(jnp.bfloat16).reshape(tok_count, heads, HD)
    pages = tok_count // PAGE
    page_kv = jnp.stack([keys, vals], 1).reshape(pages, PAGE * 2 * heads * HD)
    ngroup = lax.axis_size("group")
    myself = lax.axis_index("group")
    owners_all = page_owner[:, 0].reshape(ngroup, pages)
    owned = lax.dynamic_index_in_dim(owners_all, myself, 0, keepdims=False)
    onehot = (owned[:, None] == jnp.arange(ngroup)[None, :]).astype(jnp.float32)
    earlier = (jnp.arange(pages)[:, None] > jnp.arange(pages)[None, :]).astype(jnp.float32)
    before = jnp.dot(earlier, onehot, preferred_element_type=jnp.float32)
    rank = jnp.sum(before * onehot, 1).astype(jnp.int32)
    target = owned * CAP + rank
    chooser = (jnp.arange(ngroup * CAP)[:, None] == target[None, :]).astype(jnp.bfloat16)
    outgoing = jnp.dot(chooser, page_kv, preferred_element_type=jnp.float32).astype(jnp.bfloat16)
    outgoing = outgoing.reshape(ngroup * CAP, PAGE, 2, heads, HD)
    received = lax.all_to_all(outgoing, "group", split_axis=0, concat_axis=0, tiled=True)
    counts = jnp.sum((owners_all == myself).astype(jnp.int32), 1)
    filled = (jnp.arange(CAP)[None, :] < counts[:, None]).reshape(-1).astype(jnp.int32)
    return attend(queries, kv_cache, received, filled, cache_lengths)


def solution(mesh):
    return jax.shard_map(
        per_device,
        mesh=mesh,
        in_specs=(
            P("group", None),
            P(),
            P("group", "tensor"),
            P("group", "tensor"),
            P("group"),
            P(),
            P("group", "tensor"),
            P("group", None, None, "tensor", None),
            P("group"),
        ),
        out_specs=P("group", "tensor"),
        check_vma=False,
    )
```

profile of v0, /device:TPU:0, one launch (start us, length us, event | category | flops | bytes accessed | tf_op | source)
XLA Modules:
  0.0 213.5 jit_solution(11566136013778390777)
XLA Ops:
  6.5 0.0 all-gather.5.cloned.1.call-start
  6.5 0.7 all-gather.5.cloned.1.call-update
  7.3 0.0 all-gather.3.cloned.1.call-start
  7.3 0.7 all-gather.3.cloned.1.call-update
  8.0 0.7 convert_element_type.76
  8.7 0.5 broadcast.81
  9.2 1.3 reduce.5
  10.5 0.1 reshape_squeeze.3
  10.6 0.1 fusion.18
  10.8 0.0 copy-start.2
  10.8 5.1 %fusion = f32[512]{0:T(512)S(1)} fusion(bf16[512,8192]{1,0:T(8,128)(2,1)} %param.9), kind=kLoop, calls=%fused_computation.2 | loop fusion | flops 12582400 | bytes 8390656 | tf_op jit(solution)/shard_map/reduce_sum | solution.py:64
  15.9 1.0 multiply_cosine_fusion
  16.9 68.7 %all-gather.5.cloned.1.call-done = bf16[8192,256]{1,0:T(8,128)(2,1)} async-done(((bf16[1024,256]{1,0:T(8,128)(2,1)}), bf16[8192,256]{1,0:T(8,128)(2,1)}) %all-gather.5.cloned.1.call-update) | async-done | bytes 4194320 | tf_op jit(solution)/shard_map/all_gather | solution.py:68
  85.6 0.0 copy-done.2
  85.6 7.4 %fusion.15 = bf16[512,256]{0,1:T(8,128)(2,1)S(1)} fusion(bf16[8192,256]{1,0:T(8,128)(2,1)} %all-gather.5.cloned.1.call-done, bf16[512,8192]{1,0:T(8,128)(2,1)} %param.9, f32[8192]{0:T(1024)S(1)} %copy-done.2, f32[512]{0:T(512)S(1)} %add_rsqrt_fusion), kind=kOutput, calls=%fused_computation.19 | convolution fusion | flops 2164391936 | bytes 12879872 | tf_op jit(solution)/shard_map/dot_general | solution.py:71
  93.0 0.2 copy.24
  93.2 66.2 %all-gather.3.cloned.1.call-done = bf16[8192,256]{1,0:T(8,128)(2,1)} async-done(((bf16[1024,256]{1,0:T(8,128)(2,1)}), bf16[8192,256]{1,0:T(8,128)(2,1)}) %all-gather.3.cloned.1.call-update) | async-done | bytes 4194320 | tf_op jit(solution)/shard_map/all_gather | solution.py:67
  159.4 7.6 %fusion.5 = f32[512,256]{0,1:T(8,128)S(1)} fusion(bf16[8192,256]{1,0:T(8,128)(2,1)} %all-gather.3.cloned.1.call-done, bf16[512,8192]{1,0:T(8,128)(2,1)} %param.9, f32[8192]{0:T(1024)S(1)} %copy-done.2, f32[512]{0:T(512)S(1)} %add_rsqrt_fusion), kind=kOutput, calls=%fused_computation.7 | convolution fusion | flops 2164260864 | bytes 13142016 | tf_op jit(solution)/shard_map/dot_general | solution.py:70
  167.0 0.2 copy.31
  167.3 0.2 copy.30
  167.5 0.5 fusion.23
  168.1 1.0 pad_maximum_fusion
  169.1 0.4 reshape.159
  169.5 0.0 copy-start
  169.5 0.0 copy-start.1
  169.5 0.4 convolution_convert_fusion
  169.9 0.8 reshape.160
  170.7 1.3 copy.25
  172.0 4.4 %all-to-all-start = ((bf16[64,16,2,2,128]{4,1,3,2,0:T(8,128)(2,1)}), bf16[64,16,2,2,128]{4,1,3,2,0:T(8,128)(2,1)}, u32[]{:S(2)}, u32[]{:S(2)}) async-start(bf16[64,16,2,2,128]{4,1,3,2,0:T(8,128)(2,1)} %copy.25), calls=%async_computation | async-start | bytes 2097152 | tf_op jit(solution)/shard_map/all_to_all | solution.py:89
  176.5 0.0 copy-done
  176.5 0.1 convert_reduce_fusion
  176.6 0.1 convert_compare_fusion
  176.7 0.1 gt.28
  176.8 0.0 copy-done.1
  176.8 0.1 iota_compare_fusion.1
  176.9 4.7 %fusion.30 = (bf16[64,64,1,2,128]{4,3,2,1,0:T(2,128)(2,1)S(1)}, bf16[64,64,1,2,128]{4,3,2,1,0:T(2,128)(2,1)S(1)}) fusion(bf16[64,64,2,2,128]{4,3,2,1,0:T(2,128)(2,1)} %param.16), kind=kLoop, calls=%fused_computation.54 | loop fusion | bytes 8388608 | tf_op jit(solution)/shard_map/slice | solution.py:51
  181.6 1.3 fusion.32
  182.9 18.2 %all-to-all-done = bf16[64,16,2,2,128]{4,1,3,2,0:T(8,128)(2,1)} async-done(((bf16[64,16,2,2,128]{4,1,3,2,0:T(8,128)(2,1)}), bf16[64,16,2,2,128]{4,1,3,2,0:T(8,128)(2,1)}, u32[]{:S(2)}, u32[]{:S(2)}) %all-to-all-start) | async-done | bytes 1048608 | tf_op jit(solution)/shard_map/all_to_all | solution.py:89
  201.1 1.6 fusion.33
  202.7 0.6 fusion.25
  203.3 0.5 divide_convert_fusion
  203.8 1.4 fusion.19
  205.2 0.7 fusion.14
  205.9 0.8 copy.52
  (7 shorter events, 0.1 us)
Async XLA Ops:
  6.5 79.1 %all-gather.5.cloned.1.call-start = ((), (), s32[]{:S(2)}) async-start(), calls=%async_computation.2 | async-start | bytes 4718592 | tf_op jit(solution)/shard_map/all_gather | solution.py:68
  7.3 152.2 %all-gather.3.cloned.1.call-start = ((), (), s32[]{:S(2)}) async-start(), calls=%async_computation.1 | async-start | bytes 4718592 | tf_op jit(solution)/shard_map/all_gather | solution.py:67
  10.8 74.8 %copy-start.2 = (f32[8192]{0:T(1024)S(1)}, f32[8192]{0:T(1024)}, u32[]{:S(2)}) copy-start(f32[8192]{0:T(1024)} %param.10) | copy-start | bytes 98308
  169.5 6.9 %copy-start = (bf16[64,2048]{1,0:T(8,128)(2,1)S(1)}, bf16[64,2048]{1,0:T(8,128)(2,1)}, u32[]{:S(2)}) copy-start(bf16[64,2048]{1,0:T(8,128)(2,1)} %param.15) | copy-start | bytes 786436
  169.5 7.3 %copy-start.1 = (s32[64]{0:T(128)S(1)}, s32[64]{0:T(128)}, u32[]{:S(2)}) copy-start(s32[64]{0:T(128)} %param.17) | copy-start | bytes 772
  172.0 29.1 %all-to-all-start = ((bf16[64,16,2,2,128]{4,1,3,2,0:T(8,128)(2,1)}), bf16[64,16,2,2,128]{4,1,3,2,0:T(8,128)(2,1)}, u32[]{:S(2)}, u32[]{:S(2)}) async-start(bf16[64,16,2,2,128]{4,1,3,2,0:T(8,128)(2,1)} %copy.25), calls=%async_computation | async-start | bytes 2097152 | tf_op jit(solution)/shard_map/all_to_all | solution.py:89
Sparse Core Ops, SparseCore 0:
  9.5 76.0 all-gather.4
  87.7 71.6 all-gather.2
where the time goes:
time: 214 us; the launch traced here: 213 us
  waiting for transfers between devices  155 us (72%)
  matrix products  20.5 us (10%)
  between operations  13.6 us (6%)
  other arithmetic  11.1 us (5%)
  local copies, waits for them, and re-layouts  9.35 us (4%)
  starting transfers between devices  4.45 us (2%)
    all_gather x1, waiting for transfers between devices, per_device(): lax.all_gather(w_value, 'group', axis=0, tiled=True)  68.7 us
    all_gather x1, waiting for transfers between devices, per_device(): lax.all_gather(w_key, 'group', axis=0, tiled=True)  66.2 us
    all_to_all x1, waiting for transfers between devices, per_device(): lax.all_to_all(outgoing, 'group', split_axis=0, concat_axis=0, tiled=True)  18.2 us
    dot_general x1, matrix products, per_device(): key_sum = jnp.dot(normed, full_key, preferred_element_type=jnp.float32)  7.55 us
    dot_general x1, matrix products, per_device(): value_sum = jnp.dot(normed, full_value, preferred_element_type=jnp.float32)  7.42 us
    reduce_sum x1, other arithmetic, per_device(): factor = lax.rsqrt(jnp.mean(values * values, -1, keepdims=True) + 1e-05)  5.11 us
    slice x1, local copies, waits for them, and re-layouts, attend(): kv_cache[:, :, 1]  4.69 us
    all_to_all x1, starting transfers between devices, per_device(): lax.all_to_all(outgoing, 'group', split_axis=0, concat_axis=0, tiled=True)  4.41 us
  transfers between devices with their start and end apart: 3, of which 3 were waited for; matrix products, arithmetic and copies ran while one was open for 11% of the time, Pallas kernels for 0%

commit v1 on v0

--- a/solution.py
+++ b/solution.py
@@ -1,8 +1,11 @@
+import functools
 import math
 
 import jax
 import jax.numpy as jnp
 from jax import lax
+from jax.experimental import pallas as pl
+from jax.experimental.pallas import tpu as pltpu
 from jax.sharding import PartitionSpec as P
 
 HD = 128
@@ -92,9 +95,399 @@
     return attend(queries, kv_cache, received, filled, cache_lengths)
 
 
+MESH = pl.DeviceIdType.MESH
+VMEM_BUDGET = 56 * 2**20
+
+
+def project_kernel(
+    n_group,
+    n_tensor,
+    cut,
+    tok_ref,
+    gain_ref,
+    wk_ref,
+    wv_ref,
+    cos_ref,
+    sin_ref,
+    target_ref,
+    out_ref,
+    tok,
+    wbuf,
+    acc,
+    choose,
+    obuf,
+    tok_sem,
+    own_sem,
+    up_sem,
+    down_sem,
+    main_sem,
+    tail_up_sem,
+    tail_down_sem,
+    tail_sem,
+    xhead_send,
+    xtail_send,
+    xhead_sem,
+    page_send,
+    page_recv,
+):
+    line = n_group // 2
+    depth, cols = wk_ref.shape
+    count = tok.shape[0]
+    me = lax.axis_index("group")
+    mine = lax.axis_index("tensor")
+    z = lax.div(me, 2)
+    x = lax.rem(me, 2)
+    peer_x = 1 - x
+    peer = z * 2 + peer_x
+    head_rows = pl.ds(0, cut)
+    tail_rows = pl.ds(cut, depth - cut)
+
+    def send(src, dst, send_sem, recv_sem, group):
+        return pltpu.make_async_remote_copy(
+            src_ref=src,
+            dst_ref=dst,
+            send_sem=send_sem,
+            recv_sem=recv_sem,
+            device_id=(group, mine),
+            device_id_type=MESH,
+        )
+
+    def block(ph, zz, xx):
+        return wbuf.at[ph, zz * 2 + xx]
+
+    def main_copy(ph, zz, up, src=None):
+        src = block(ph, zz, x) if src is None else src
+        sem, to = (up_sem, me + 2) if up else (down_sem, me - 2)
+        return send(src, block(ph, zz, x), sem.at[ph, zz], main_sem.at[ph, zz], to)
+
+    def tail_copy(ph, zz, up):
+        part = wbuf.at[ph, zz * 2 + peer_x, tail_rows]
+        sem, to = (tail_up_sem, me + 2) if up else (tail_down_sem, me - 2)
+        return send(part, part, sem.at[ph, zz], tail_sem.at[ph, zz], to)
+
+    def xhead_copy(ph, zz, column):
+        part = wbuf.at[ph, zz * 2 + column, head_rows]
+        return send(part, part, xhead_send.at[ph, zz], xhead_sem.at[ph, zz], peer)
+
+    def xtail_copy(ph, column):
+        part = wbuf.at[ph, z * 2 + column, tail_rows]
+        return send(part, part, xtail_send.at[ph], tail_sem.at[ph, z], peer)
+
+    def both_ways(make):
+        @pl.when(z < line - 1)
+        def _():
+            make(True)
+
+        @pl.when(z > 0)
+        def _():
+            make(False)
+
+    weights = (wv_ref, wk_ref)
+
+    def own_load(ph):
+        return pltpu.make_async_copy(weights[ph], wbuf.at[ph, me], own_sem.at[ph])
+
+    def start_own(ph):
+        both_ways(lambda up: main_copy(ph, z, up).start())
+        xtail_copy(ph, x).start()
+        xhead_copy(ph, z, x).start()
+
+    def pass_own_tail(ph):
+        xtail_copy(ph, peer_x).wait_recv()
+        both_ways(lambda up: tail_copy(ph, z, up).start())
+
+    own_load(0).start()
+    own_load(1).start()
+    tok_load = pltpu.make_async_copy(tok_ref, tok, tok_sem)
+    tok_load.start()
+
+    barrier = pltpu.get_barrier_semaphore()
+    for step in range(1, n_group):
+        pl.semaphore_signal(
+            barrier,
+            inc=1,
+            device_id=(lax.rem(me + step, n_group), mine),
+            device_id_type=MESH,
+        )
+    pl.semaphore_wait(barrier, n_group - 1)
+
+    own_load(0).wait()
+    start_own(0)
+    acc[...] = jnp.zeros_like(acc)
+    own_load(1).wait()
+    tok_load.wait()
+
+    chunk = 32
+    width = tok.shape[1]
+    piece = 1024
+
+    @pl.loop(0, count // chunk)
+    def _(i):
+        rows = pl.ds(pl.multiple_of(i * chunk, chunk), chunk)
+        total = jnp.zeros((chunk, 128), jnp.float32)
+        for k in range(width // piece):
+            part = tok[rows, k * piece : (k + 1) * piece].astype(jnp.float32)
+            part = part * part
+            for j in range(piece // 128):
+                total = total + part[:, j * 128 : (j + 1) * 128]
+        mean = jnp.sum(total, -1, keepdims=True) * (1.0 / width)
+        factor = lax.rsqrt(mean + 1e-05)
+        for k in range(width // piece):
+            span = slice(k * piece, (k + 1) * piece)
+            part = tok[rows, span].astype(jnp.float32) * factor * gain_ref[:, span]
+            tok[rows, span] = part.astype(jnp.bfloat16)
+
+    pass_own_tail(0)
+
+    slots = choose.shape[0]
+
+    @pl.loop(0, slots // 128)
+    def _(i):
+        start = pl.multiple_of(i * 128, 128)
+        row = lax.broadcasted_iota(jnp.int32, (128, count), 0) + start
+        hit = row == target_ref[...]
+        choose[pl.ds(start, 128), :] = jnp.where(hit, 1.0, 0.0).astype(jnp.bfloat16)
+
+    half = count // 2
+
+    def multiply(ph, index):
+        span = pl.ds(pl.multiple_of(index * depth, depth), depth)
+
+        @pl.loop(0, 2)
+        def _(i):
+            rows = pl.ds(pl.multiple_of(i * half, half), half)
+            acc[ph, rows, :] += jnp.dot(
+                tok[rows, span], wbuf[ph, index], preferred_element_type=jnp.float32
+            )
+
+    per_owner = slots // n_group
+
+    def page_copy(ph, step):
+        to = lax.rem(me + step, n_group)
+        return send(
+            obuf.at[ph, to], out_ref.at[ph, me], page_send.at[ph, to], page_recv.at[ph, me], to
+        )
+
+    def page_wait(ph, step):
+        origin = lax.rem(me + step, n_group)
+        send(
+            obuf.at[ph, origin],
+            out_ref.at[ph, origin],
+            page_send.at[ph, origin],
+            page_recv.at[ph, origin],
+            origin,
+        ).wait_recv()
+
+    def hand_over(ph):
+        held = acc[ph]
+        if ph == 1:
+            turned = [
+                held[:, s : s + HD] * cos_ref[...]
+                + pltpu.roll(held[:, s : s + HD], HD // 2, 1) * sin_ref[...]
+                for s in range(0, cols, HD)
+            ]
+            held = jnp.concatenate(turned, -1)
+        held = held.astype(jnp.bfloat16)
+
+        for owner in range(n_group):
+            rows = choose[owner * per_owner : (owner + 1) * per_owner, :]
+            picked = jnp.dot(rows, held, preferred_element_type=jnp.float32)
+            obuf[ph, owner] = picked.astype(jnp.bfloat16)
+        for step in range(1, n_group):
+            page_copy(ph, step).start()
+        out_ref[ph, me] = obuf[ph, me]
+
+    def at(step, way):
+        ph = lax.div(step, line)
+        dist = lax.rem(step, line)
+        zz = z + dist * (2 * way - 1)
+        live = (zz >= 0) & (zz < line) & ((dist > 0) | (way == 0))
+        return ph, dist, zz, live
+
+    def forward(ph, dist, zz, way, copy):
+        @pl.when((way == 0) & (z < line - 1))
+        def _():
+            copy(ph, zz, True).start()
+
+        @pl.when((way == 1) & (z > 0))
+        def _():
+            copy(ph, zz, False).start()
+
+    @pl.loop(0, 2 * line + 1)
+    def _(step):
+        @pl.when(step < 2 * line)
+        def _():
+            @pl.loop(0, 2)
+            def _(way):
+                ph, dist, zz, live = at(step, way)
+
+                @pl.when(live & (dist > 0))
+                def _():
+                    main_copy(ph, zz, True).wait_recv()
+                    forward(ph, dist, zz, way, main_copy)
+                    xhead_copy(ph, zz, x).start()
+
+            @pl.loop(0, 2)
+            def _(way):
+                ph, dist, zz, live = at(step, way)
+
+                @pl.when(live & (dist > 0))
+                def _():
+                    tail_copy(ph, zz, True).wait_recv()
+                    forward(ph, dist, zz, way, tail_copy)
+
+            @pl.when(step == 1)
+            def _():
+                start_own(1)
+
+            @pl.when(step == 2)
+            def _():
+                pass_own_tail(1)
+
+            @pl.loop(0, 2)
+            def _(way):
+                ph, dist, zz, live = at(step, way)
+
+                @pl.when(live)
+                def _():
+                    multiply(ph, zz * 2 + x)
+
+        @pl.when(step > 0)
+        def _():
+            @pl.loop(0, 2)
+            def _(way):
+                ph, dist, zz, live = at(step - 1, way)
+
+                @pl.when(live)
+                def _():
+                    xhead_copy(ph, zz, peer_x).wait_recv()
+                    multiply(ph, zz * 2 + peer_x)
+
+        @pl.when(step == line)
+        def _():
+            hand_over(0)
+
+    hand_over(1)
+
+    for ph in range(2):
+        xtail_copy(ph, x).wait_send()
+        for zz in range(line):
+            xhead_copy(ph, zz, x).wait_send()
+
+            @pl.when((z < line - 1) & (zz <= z))
+            def _():
+                main_copy(ph, zz, True).wait_send()
+                tail_copy(ph, zz, True).wait_send()
+
+            @pl.when((z > 0) & (zz >= z))
+            def _():
+                main_copy(ph, zz, False).wait_send()
+                tail_copy(ph, zz, False).wait_send()
+
+        for step in range(1, n_group):
+            page_copy(ph, step).wait_send()
+            page_wait(ph, step)
+
+
+def project(n_group, n_tensor, tokens, norm_gain, w_key, w_value, cosine, sine, target):
+    count, width = tokens.shape
+    depth, cols = w_key.shape
+    line = n_group // 2
+    slots = n_group * CAP * PAGE
+    cut = depth - depth // 8
+    vmem = pl.BlockSpec(memory_space=pltpu.VMEM)
+    hbm = pl.BlockSpec(memory_space=pl.ANY)
+    dma = pltpu.SemaphoreType.DMA
+    return pl.pallas_call(
+        functools.partial(project_kernel, n_group, n_tensor, cut),
+        out_shape=jax.ShapeDtypeStruct((2, n_group, slots // n_group, cols), jnp.bfloat16),
+        in_specs=[hbm, vmem, hbm, hbm, vmem, vmem, vmem],
+        out_specs=vmem,
+        scratch_shapes=[
+            pltpu.VMEM((count, width), jnp.bfloat16),
+            pltpu.VMEM((2, n_group, depth, cols), jnp.bfloat16),
+            pltpu.VMEM((2, count, cols), jnp.float32),
+            pltpu.VMEM((slots, count), jnp.bfloat16),
+            pltpu.VMEM((2, n_group, slots // n_group, cols), jnp.bfloat16),
+            dma,
+            dma((2,)),
+            dma((2, line)),
+            dma((2, line)),
+            dma((2, line)),
+            dma((2, line)),
+            dma((2, line)),
+            dma((2, line)),
+            dma((2, line)),
+            dma((2,)),
+            dma((2, line)),
+            dma((2, n_group)),
+            dma((2, n_group)),
+        ],
+        compiler_params=pltpu.CompilerParams(
+            collective_id=0, has_side_effects=True, vmem_limit_bytes=VMEM_BUDGET
+        ),
+        cost_estimate=pl.CostEstimate(
+            flops=4 * count * width * cols,
+            bytes_accessed=2 * count * width + 4 * depth * cols,
+            transcendentals=0,
+        ),
+    )(tokens, norm_gain[None, :], w_key, w_value, cosine, sine, target)
+
+
+def page_targets(page_owner, ngroup, pages, myself):
+    owners_all = page_owner[:, 0].reshape(ngroup, pages)
+    owned = lax.dynamic_index_in_dim(owners_all, myself, 0, keepdims=False)
+    earlier = jnp.arange(pages)[:, None] > jnp.arange(pages)[None, :]
+    same = owned[:, None] == owned[None, :]
+    rank = jnp.sum((earlier & same).astype(jnp.int32), 1)
+    counts = jnp.sum((owners_all == myself).astype(jnp.int32), 1)
+    filled = (jnp.arange(CAP)[None, :] < counts[:, None]).reshape(-1).astype(jnp.int32)
+    return owned * CAP + rank, filled
+
+
+def per_device_fused(
+    tokens, norm_gain, w_key, w_value, positions, page_owner, queries, kv_cache, cache_lengths
+):
+    count = tokens.shape[0]
+    pages = count // PAGE
+    ngroup = lax.axis_size("group")
+    ntensor = lax.axis_size("tensor")
+    myself = lax.axis_index("group")
+    index = jnp.arange(HD // 2).astype(jnp.float32)
+    inverse = jnp.exp(index * (-2.0 * math.log(500000.0) / HD))
+    angles = positions.astype(jnp.float32)[:, None] * inverse[None, :]
+    cosine, sine = jnp.cos(angles), jnp.sin(angles)
+    cosine = jnp.concatenate([cosine, cosine], -1)
+    sine = jnp.concatenate([-sine, sine], -1)
+    target, filled = page_targets(page_owner, ngroup, pages, myself)
+    rows = (target[:, None] * PAGE + jnp.arange(PAGE)[None, :]).reshape(1, count)
+    placed = project(
+        ngroup, ntensor, tokens, norm_gain, w_key, w_value, cosine, sine, rows
+    )
+    heads = w_key.shape[1] // HD
+    placed = placed.reshape(2, ngroup * CAP, PAGE, heads, HD)
+    received = jnp.stack([placed[1], placed[0]], 2)
+    return attend(queries, kv_cache, received, filled, cache_lengths)
+
+
+def fits(count, width, cols, ngroup):
+    slots = ngroup * CAP * PAGE
+    held = 2 * count * width + 4 * width * cols + 8 * count * cols
+    held += 2 * slots * count + 8 * slots * cols + 8 * count * HD
+    return 3 * held < 2 * VMEM_BUDGET
+
+
+def pick(tokens, norm_gain, w_key, *rest):
+    ngroup = lax.axis_size("group")
+    count, width = tokens.shape
+    fused = ngroup % 2 == 0 and count % 256 == 0 and w_key.shape[0] % 1024 == 0
+    fused = fused and fits(count, width, w_key.shape[1], ngroup)
+    return (per_device_fused if fused else per_device)(tokens, norm_gain, w_key, *rest)
+
+
 def solution(mesh):
     return jax.shard_map(
-        per_device,
+        pick,
         mesh=mesh,
         in_specs=(
             P("group", None),

time: 214 us -> 136 us (0.64)
  waiting for transfers between devices: 155 us -> 0 us
  Pallas kernels: 0 us -> 116 us
  matrix products: 20.5 us -> 2.9 us
  between operations: 13.6 us -> 0.11 us
  other arithmetic: 11.1 us -> 5.02 us
  starting transfers between devices: 4.45 us -> 0 us
    all_gather x2 -> x0, waiting for transfers between devices: 135 us -> none  [the longest x1 68.7 us: per_device(): lax.all_gather(w_value, 'group', axis=0, tiled=True)]
    pallas_call x0 -> x1, Pallas kernels: none -> 116 us  [project(): pl.pallas_call(functools.partial(project_kernel, n_group, n_tensor, cut),...]
    all_to_all x1 -> x0, waiting for transfers between devices: 18.2 us -> none  [per_device(): lax.all_to_all(outgoing, 'group', split_axis=0, concat_axis=0, tiled=True)]
    dot_general x4 -> x0, matrix products: 15.5 us -> none  [the longest x1 7.55 us: per_device(): key_sum = jnp.dot(normed, full_key, preferred_element_type=jnp.float32)]
    reduce_sum x2, other arithmetic: 5.23 us -> 0.3 us  [the longest x1 0.18 us: page_targets(): rank = jnp.sum((earlier & same).astype(jnp.int32), 1)]
    all_to_all x1 -> x0, starting transfers between devices: 4.41 us -> none  [per_device(): lax.all_to_all(outgoing, 'group', split_axis=0, concat_axis=0, tiled=True)]
    reshape x3 -> x0, local copies, waits for them, and re-layouts: 2.48 us -> none  [the longest x2 2.08 us: per_device(): outgoing = outgoing.reshape(ngroup * CAP, PAGE, 2, heads, HD)]
  transfers between devices with their start and end apart: 3 -> 0, of which waited for: 3 -> 0; matrix products, arithmetic and copies ran while one was open for 11% -> 0% of each run, Pallas kernels for 0% -> 0%
where the time goes in v1:
time: 136 us; the launch traced here: 135 us
  Pallas kernels  116 us (85%)
  local copies, waits for them, and re-layouts  11.2 us (8%)
  other arithmetic  5.02 us (4%)
  matrix products  2.9 us (2%)
    pallas_call x1, Pallas kernels, project(): pl.pallas_call(functools.partial(project_kernel, n_group, n_tensor, cut),...  116 us
    slice x1, local copies, waits for them, and re-layouts, attend(): kv_cache[:, :, 1]  4.69 us

profile of v1, /device:TPU:0, one launch (start us, length us, event | category | flops | bytes accessed | tf_op | source)
XLA Modules:
  0.0 135.4 jit_solution(3162155392128405189)
XLA Ops:
  0.0 0.0 copy-start.2
  0.0 0.7 convert_element_type.39
  0.7 1.0 fusion.14
  1.7 1.0 pad_maximum_fusion
  2.7 0.6 broadcast.49
  3.3 0.0 copy-done.2
  3.3 0.7 reduce.5
  4.0 0.1 reshape_squeeze.3
  4.1 0.2 convert_reduce_fusion
  4.3 0.1 iota_add_fusion
  4.4 0.7 add.42.target_ref
  5.0 116.2 %shard_map.91 = bf16[2,8,128,256]{3,2,1,0:T(8,128)(2,1)} custom-call(bf16[512,8192]{1,0:T(8,128)(2,1)} %tok_ref.1, f32[1,8192]{1,0:T(1,128)} %bitcast.42, bf16[1024,256]{1,0:T(8,128)(2,1)} %wk_ref.1, bf16[1024,256]{1,0:T(8,128)(2,1)} %wv_ref.1, f32[512,128]{1,0:T(8,128)} %get-tuple-element.16.cos_ref, f32[512,128]{1,0:T(8,128)} %get-tuple-element.17.sin_ref, ...), custom_call_target="tpu_custom_call" | custom-call | flops 4294967296 | bytes 9437184 | tf_op jit(solution)/shard_map/pallas_call | solution.py:401
  121.2 0.0 copy-start.1
  121.2 2.1 %fusion.18 = (bf16[1,8,128,256]{3,2,1,0:T(8,128)(2,1)}, bf16[1,8,128,256]{3,2,1,0:T(8,128)(2,1)S(1)}) fusion(bf16[2,8,128,256]{3,2,1,0:T(8,128)(2,1)} %shard_map.91), kind=kLoop, calls=%fused_computation.38 | loop fusion | bytes 2097152 | tf_op jit(solution)/shard_map/slice | solution.py:469
  123.4 0.9 squeeze_stack_squeeze.7
  124.3 0.0 copy-done.1
  124.3 0.0 copy-start.3
  124.3 4.7 %fusion.17 = (bf16[64,64,1,2,128]{4,3,2,1,0:T(2,128)(2,1)S(1)}, bf16[64,64,1,2,128]{4,3,2,1,0:T(2,128)(2,1)S(1)}) fusion(bf16[64,64,2,2,128]{4,3,2,1,0:T(2,128)(2,1)} %param.16), kind=kLoop, calls=%fused_computation.37 | loop fusion | bytes 8388608 | tf_op jit(solution)/shard_map/slice | solution.py:54
  129.0 0.0 copy-done.3
  129.0 0.1 iota_compare_fusion
  129.1 1.3 fusion.19
  130.5 1.2 squeeze_stack_squeeze.6
  131.6 0.1 convert_reduce_fusion.1
  131.7 0.1 convert_compare_fusion
  131.8 0.1 gt.28
  131.9 0.0 copy-start
  131.9 0.6 fusion.20
  132.5 0.6 fusion.15
  133.1 0.5 divide_convert_fusion
  133.6 0.0 copy-done
  133.6 0.3 fusion.9
  133.9 0.7 fusion.7
  134.6 0.8 copy.47
  (5 shorter events, 0.1 us)
Async XLA Ops:
  0.0 3.3 %copy-start.2 = (s32[256,1]{0,1:T(1,128)S(1)}, s32[256,1]{0,1:T(1,128)}, u32[]{:S(2)}) copy-start(s32[256,1]{0,1:T(1,128)} %param.14) | copy-start | bytes 3076
  121.2 3.1 %copy-start.1 = (bf16[64,2048]{1,0:T(8,128)(2,1)S(1)}, bf16[64,2048]{1,0:T(8,128)(2,1)}, u32[]{:S(2)}) copy-start(bf16[64,2048]{1,0:T(8,128)(2,1)} %param.15) | copy-start | bytes 786436
  124.3 4.7 %copy-start.3 = (s32[64]{0:T(128)S(1)}, s32[64]{0:T(128)}, u32[]{:S(2)}) copy-start(s32[64]{0:T(128)} %param.17) | copy-start | bytes 772
  131.9 1.7 %copy-start = (bf16[64,16,2,128]{3,2,1,0:T(2,128)(2,1)S(1)}, bf16[64,16,2,128]{3,2,1,0:T(2,128)(2,1)}, u32[]{:S(2)}) copy-start(bf16[64,16,2,128]{3,2,1,0:T(2,128)(2,1)} %squeeze_stack_squeeze.7) | copy-start | bytes 1572868

commit v2 on v1

--- a/solution.py
+++ b/solution.py
@@ -101,22 +101,34 @@
 
 def project_kernel(
     n_group,
-    n_tensor,
     cut,
     tok_ref,
     gain_ref,
     wk_ref,
     wv_ref,
-    cos_ref,
-    sin_ref,
-    target_ref,
+    pos_ref,
+    owner_ref,
+    query_ref,
+    cache_ref,
+    length_ref,
     out_ref,
     tok,
     wbuf,
     acc,
     choose,
     obuf,
+    rbuf,
+    cos_ref,
+    sin_ref,
+    cache,
+    query_f,
+    query_b,
+    near_out,
+    near_max,
+    near_sum,
+    result,
     tok_sem,
+    cache_sem,
     own_sem,
     up_sem,
     down_sem,
@@ -200,6 +212,8 @@
     own_load(1).start()
     tok_load = pltpu.make_async_copy(tok_ref, tok, tok_sem)
     tok_load.start()
+    cache_load = pltpu.make_async_copy(cache_ref, cache, cache_sem)
+    cache_load.start()
 
     barrier = pltpu.get_barrier_semaphore()
     for step in range(1, n_group):
@@ -240,13 +254,128 @@
     pass_own_tail(0)
 
     slots = choose.shape[0]
+    owned_pages = count // PAGE
+    every = owner_ref.shape[1]
+
+    def grid_of(shape, dim):
+        return lax.broadcasted_iota(jnp.int32, shape, dim)
+
+    def column(row):
+        size = row.shape[1]
+        same = grid_of((size, size), 0) == grid_of((size, size), 1)
+        return jnp.sum(jnp.where(same, row, 0), 1, keepdims=True)
+
+    owner_row = owner_ref[...].astype(jnp.float32)
+    owner_col = column(owner_row)
+    first = grid_of((every, every), 0)
+    second = grid_of((every, every), 1)
+    before = (owner_col == owner_row) & (first < second)
+    before = before & (first // owned_pages == second // owned_pages)
+    rank = jnp.sum(jnp.where(before, 1.0, 0.0), 0, keepdims=True)
+    place = owner_row * CAP + rank
+    page_of = grid_of((every, count), 0) == me * owned_pages + grid_of((every, count), 1) // PAGE
+    place_col = column(place)
+    token_place = jnp.sum(jnp.where(page_of, place_col, 0.0), 0, keepdims=True)
+    token_row = token_place.astype(jnp.int32) * PAGE + grid_of((1, count), 1) % PAGE
+
+    lane = grid_of((1, HD), 1)
+    index = (lane % (HD // 2)).astype(jnp.float32)
+    inverse = jnp.exp(index * (-2.0 * math.log(500000.0) / HD))
+    for start in range(0, count, 128):
+        angles = column(pos_ref[:, start : start + 128].astype(jnp.float32)) * inverse
+        cos_ref[start : start + 128, :] = jnp.cos(angles)
+        turn = jnp.sin(angles)
+        sin_ref[start : start + 128, :] = jnp.where(lane < HD // 2, -turn, turn)
 
     @pl.loop(0, slots // 128)
     def _(i):
         start = pl.multiple_of(i * 128, 128)
         row = lax.broadcasted_iota(jnp.int32, (128, count), 0) + start
-        hit = row == target_ref[...]
+        hit = row == token_row
         choose[pl.ds(start, 128), :] = jnp.where(hit, 1.0, 0.0).astype(jnp.bfloat16)
+
+    query_f[...] = query_ref[...].astype(jnp.float32)
+    heads = query_f.shape[1] // HD
+    kv_heads = cols // HD
+    share = heads // kv_heads
+    group_rows = heads * CAP
+    span_rows = cache.shape[0] // n_group
+    live_span = span_rows // (CAP * 2 * kv_heads)
+    scale = 1.0 / math.sqrt(HD)
+    row_id = grid_of((group_rows, 1), 0)
+    row_slot = row_id % CAP
+    row_head = row_id // (CAP * share)
+    cache_load.wait()
+
+    def near(i):
+        base = pl.multiple_of(i * CAP, CAP)
+        parts = [query_f[pl.ds(base, CAP), j * HD : (j + 1) * HD] for j in range(heads)]
+        asked = jnp.concatenate(parts, 0).astype(jnp.bfloat16)
+        rows = pl.ds(pl.multiple_of(i * group_rows, group_rows), group_rows)
+        query_b[rows, :] = asked
+        entries = cache[pl.ds(pl.multiple_of(i * span_rows, span_rows), span_rows), :]
+        scores = lax.dot_general(
+            asked, entries, (((1,), (1,)), ((), ())), preferred_element_type=jnp.float32
+        )
+        col = grid_of((1, span_rows), 1)
+        width_l = 2 * kv_heads
+        col_head = col % kv_heads
+        col_code = (col // (width_l * live_span)) * kv_heads + col_head
+        col_code = jnp.where((col % width_l) < kv_heads, col_code, -1)
+        col_pos = (col // width_l) % live_span
+        lengths = length_ref[...]
+        which = grid_of((group_rows, lengths.shape[1]), 1) == i * CAP + row_slot
+        limit = jnp.sum(jnp.where(which, lengths, 0), 1, keepdims=True)
+        ok = (col_code == row_slot * kv_heads + row_head) & (col_pos < limit)
+        scores = jnp.where(ok, scores * scale, -1e30)
+        top = jnp.max(scores, 1, keepdims=True)
+        weights = jnp.exp(scores - top)
+        total = jnp.sum(weights, 1, keepdims=True)
+        moved = pltpu.roll(weights, kv_heads, 1).astype(jnp.bfloat16)
+        near_out[rows, :] = jnp.dot(moved, entries, preferred_element_type=jnp.float32)
+        near_max[rows, :] = jnp.broadcast_to(top, (group_rows, HD))
+        near_sum[rows, :] = jnp.broadcast_to(total, (group_rows, HD))
+
+    def fresh(i):
+        rows = slice(i * group_rows, (i + 1) * group_rows)
+        each = group_rows // kv_heads
+        found = []
+        for h in range(kv_heads):
+            asked = query_b[i * group_rows + h * each : i * group_rows + (h + 1) * each, :]
+            found.append(
+                lax.dot_general(
+                    asked,
+                    rbuf[1, i, :, h * HD : (h + 1) * HD],
+                    (((1,), (1,)), ((), ())),
+                    preferred_element_type=jnp.float32,
+                )
+            )
+        scores = jnp.concatenate(found, 0)
+        page = grid_of((1, every), 1) // owned_pages
+        sent = (owner_row == me.astype(jnp.float32)) & (page == i)
+        number = jnp.sum(jnp.where(sent, 1.0, 0.0), 1, keepdims=True)
+        slot = grid_of((1, CAP * PAGE), 1) // PAGE
+        ok = (slot == row_slot) & (slot.astype(jnp.float32) < number)
+        scores = jnp.where(ok, scores * scale, -1e30)
+        old_top = near_max[rows, :]
+        top = jnp.maximum(jnp.max(scores, 1, keepdims=True), old_top)
+        weights = jnp.where(ok, jnp.exp(scores - top), 0.0)
+        keep = jnp.exp(old_top - top)
+        total = near_sum[rows, :] * keep + jnp.sum(weights, 1, keepdims=True)
+        weights = weights.astype(jnp.bfloat16)
+        mixed = [
+            jnp.dot(
+                weights[h * each : (h + 1) * each, :],
+                rbuf[0, i, :, h * HD : (h + 1) * HD],
+                preferred_element_type=jnp.float32,
+            )
+            for h in range(kv_heads)
+        ]
+        final = (near_out[rows, :] * keep + jnp.concatenate(mixed, 0)) / total
+        for j in range(heads):
+            result[i * CAP : (i + 1) * CAP, j * HD : (j + 1) * HD] = final[
+                j * CAP : (j + 1) * CAP, :
+            ]
 
     half = count // 2
 
@@ -265,14 +394,14 @@
     def page_copy(ph, step):
         to = lax.rem(me + step, n_group)
         return send(
-            obuf.at[ph, to], out_ref.at[ph, me], page_send.at[ph, to], page_recv.at[ph, me], to
+            obuf.at[ph, to], rbuf.at[ph, me], page_send.at[ph, to], page_recv.at[ph, me], to
         )
 
     def page_wait(ph, step):
         origin = lax.rem(me + step, n_group)
         send(
             obuf.at[ph, origin],
-            out_ref.at[ph, origin],
+            rbuf.at[ph, origin],
             page_send.at[ph, origin],
             page_recv.at[ph, origin],
             origin,
@@ -295,7 +424,7 @@
             obuf[ph, owner] = picked.astype(jnp.bfloat16)
         for step in range(1, n_group):
             page_copy(ph, step).start()
-        out_ref[ph, me] = obuf[ph, me]
+        rbuf[ph, me] = obuf[ph, me]
 
     def at(step, way):
         ph = lax.div(step, line)
@@ -352,6 +481,8 @@
                 def _():
                     multiply(ph, zz * 2 + x)
 
+            near(step)
+
         @pl.when(step > 0)
         def _():
             @pl.loop(0, 2)
@@ -368,6 +499,12 @@
             hand_over(0)
 
     hand_over(1)
+    for ph in range(2):
+        for step in range(1, n_group):
+            page_wait(ph, step)
+    for i in range(n_group):
+        fresh(i)
+    out_ref[...] = result[...].astype(jnp.bfloat16)
 
     for ph in range(2):
         xtail_copy(ph, x).wait_send()
@@ -386,29 +523,46 @@
 
         for step in range(1, n_group):
             page_copy(ph, step).wait_send()
-            page_wait(ph, step)
-
-
-def project(n_group, n_tensor, tokens, norm_gain, w_key, w_value, cosine, sine, target):
+
+
+def per_device_fused(
+    tokens, norm_gain, w_key, w_value, positions, page_owner, queries, kv_cache, cache_lengths
+):
     count, width = tokens.shape
     depth, cols = w_key.shape
+    n_group = lax.axis_size("group")
     line = n_group // 2
     slots = n_group * CAP * PAGE
     cut = depth - depth // 8
+    rows = queries.shape[0]
+    asked = rows * queries.shape[1] // HD
+    cache = kv_cache.reshape(-1, HD)
     vmem = pl.BlockSpec(memory_space=pltpu.VMEM)
     hbm = pl.BlockSpec(memory_space=pl.ANY)
     dma = pltpu.SemaphoreType.DMA
+    f32, bf16 = jnp.float32, jnp.bfloat16
     return pl.pallas_call(
-        functools.partial(project_kernel, n_group, n_tensor, cut),
-        out_shape=jax.ShapeDtypeStruct((2, n_group, slots // n_group, cols), jnp.bfloat16),
-        in_specs=[hbm, vmem, hbm, hbm, vmem, vmem, vmem],
+        functools.partial(project_kernel, n_group, cut),
+        out_shape=jax.ShapeDtypeStruct(queries.shape, bf16),
+        in_specs=[hbm, vmem, hbm, hbm, vmem, vmem, vmem, hbm, vmem],
         out_specs=vmem,
         scratch_shapes=[
-            pltpu.VMEM((count, width), jnp.bfloat16),
-            pltpu.VMEM((2, n_group, depth, cols), jnp.bfloat16),
-            pltpu.VMEM((2, count, cols), jnp.float32),
-            pltpu.VMEM((slots, count), jnp.bfloat16),
-            pltpu.VMEM((2, n_group, slots // n_group, cols), jnp.bfloat16),
+            pltpu.VMEM((count, width), bf16),
+            pltpu.VMEM((2, n_group, depth, cols), bf16),
+            pltpu.VMEM((2, count, cols), f32),
+            pltpu.VMEM((slots, count), bf16),
+            pltpu.VMEM((2, n_group, slots // n_group, cols), bf16),
+            pltpu.VMEM((2, n_group, slots // n_group, cols), bf16),
+            pltpu.VMEM((count, HD), f32),
+            pltpu.VMEM((count, HD), f32),
+            pltpu.VMEM(cache.shape, bf16),
+            pltpu.VMEM(queries.shape, f32),
+            pltpu.VMEM((asked, HD), bf16),
+            pltpu.VMEM((asked, HD), f32),
+            pltpu.VMEM((asked, HD), f32),
+            pltpu.VMEM((asked, HD), f32),
+            pltpu.VMEM(queries.shape, f32),
+            dma,
             dma,
             dma((2,)),
             dma((2, line)),
@@ -431,43 +585,17 @@
             bytes_accessed=2 * count * width + 4 * depth * cols,
             transcendentals=0,
         ),
-    )(tokens, norm_gain[None, :], w_key, w_value, cosine, sine, target)
-
-
-def page_targets(page_owner, ngroup, pages, myself):
-    owners_all = page_owner[:, 0].reshape(ngroup, pages)
-    owned = lax.dynamic_index_in_dim(owners_all, myself, 0, keepdims=False)
-    earlier = jnp.arange(pages)[:, None] > jnp.arange(pages)[None, :]
-    same = owned[:, None] == owned[None, :]
-    rank = jnp.sum((earlier & same).astype(jnp.int32), 1)
-    counts = jnp.sum((owners_all == myself).astype(jnp.int32), 1)
-    filled = (jnp.arange(CAP)[None, :] < counts[:, None]).reshape(-1).astype(jnp.int32)
-    return owned * CAP + rank, filled
-
-
-def per_device_fused(
-    tokens, norm_gain, w_key, w_value, positions, page_owner, queries, kv_cache, cache_lengths
-):
-    count = tokens.shape[0]
-    pages = count // PAGE
-    ngroup = lax.axis_size("group")
-    ntensor = lax.axis_size("tensor")
-    myself = lax.axis_index("group")
-    index = jnp.arange(HD // 2).astype(jnp.float32)
-    inverse = jnp.exp(index * (-2.0 * math.log(500000.0) / HD))
-    angles = positions.astype(jnp.float32)[:, None] * inverse[None, :]
-    cosine, sine = jnp.cos(angles), jnp.sin(angles)
-    cosine = jnp.concatenate([cosine, cosine], -1)
-    sine = jnp.concatenate([-sine, sine], -1)
-    target, filled = page_targets(page_owner, ngroup, pages, myself)
-    rows = (target[:, None] * PAGE + jnp.arange(PAGE)[None, :]).reshape(1, count)
-    placed = project(
-        ngroup, ntensor, tokens, norm_gain, w_key, w_value, cosine, sine, rows
-    )
-    heads = w_key.shape[1] // HD
-    placed = placed.reshape(2, ngroup * CAP, PAGE, heads, HD)
-    received = jnp.stack([placed[1], placed[0]], 2)
-    return attend(queries, kv_cache, received, filled, cache_lengths)
+    )(
+        tokens,
+        norm_gain[None, :],
+        w_key,
+        w_value,
+        positions[None, :],
+        page_owner.reshape(1, -1),
+        queries,
+        cache,
+        cache_lengths[None, :],
+    )
 
 
 def fits(count, width, cols, ngroup):

time: 136 us -> 122 us (0.90)
  local copies, waits for them, and re-layouts: 11.2 us -> 1.67 us
  other arithmetic: 5.02 us -> 0 us
  Pallas kernels: 116 us -> 120 us
  matrix products: 2.9 us -> 0 us
    slice x2 -> x0, local copies, waits for them, and re-layouts: 6.84 us -> none  [the longest x1 4.69 us: attend(): kv_cache[:, :, 1]]
    pallas_call x1, Pallas kernels: 116 us -> 120 us  [per_device_fused(): pl.pallas_call(functools.partial(project_kernel, n_group, cut), out_shape...]
    dot_general x4 -> x0, matrix products: 2.9 us -> none  [the longest x1 1.33 us: attend(): jnp.einsum('rhgd,rlhd->rhgl', query_b, kv_cache[:, :, 0], preferred_eleme...]
    another operation x3 -> x0, local copies, waits for them, and re-layouts: 2.16 us -> none  [the longest x1 1.17 us: attend(): placed[:, :, 0]]
where the time goes in v2:
time: 122 us
  Pallas kernels  120 us (98%)
  local copies, waits for them, and re-layouts  1.67 us (1%)
    pallas_call x1, Pallas kernels, per_device_fused(): pl.pallas_call(functools.partial(project_kernel, n_group, cut), out_shape...  120 us

profile of v2, /device:TPU:0, one launch (start us, length us, event | category | flops | bytes accessed | tf_op | source)
XLA Modules:
  0.0 121.6 jit_solution(547515088385660579)
XLA Ops:
  0.0 119.9 %shard_map.91 = bf16[64,2048]{1,0:T(8,128)(2,1)} custom-call(bf16[512,8192]{1,0:T(8,128)(2,1)} %tok_ref.1, f32[1,8192]{1,0:T(1,128)} %bitcast.6, bf16[1024,256]{1,0:T(8,128)(2,1)} %wk_ref.1, bf16[1024,256]{1,0:T(8,128)(2,1)} %wv_ref.1, s32[1,512]{1,0:T(1,128)} %bitcast.7, s32[1,256]{1,0:T(1,128)} %bitcast.8, bf16[64,2048]{1,0:T(8,128)(2,1)} %query_ref.1, ...), custom_call_target="tpu_custom_call" | custom-call | flops 4294967296 | bytes 9437184 | tf_op jit(solution)/shard_map/pallas_call | solution.py:544
  119.9 1.7 %copy.11 = bf16[64,2048]{1,0:T(8,128)(2,1)} copy(bf16[64,2048]{1,0:T(8,128)(2,1)} %shard_map.91) | data formatting | bytes 524288

commit v3 on v2

--- a/solution.py
+++ b/solution.py
@@ -97,6 +97,8 @@
 
 MESH = pl.DeviceIdType.MESH
 VMEM_BUDGET = 56 * 2**20
+TAIL_LAG = 2
+PEER_LAG = 5
 
 
 def project_kernel(
@@ -194,10 +196,14 @@
         def _():
             make(False)
 
-    weights = (wv_ref, wk_ref)
+    kv_heads = cols // HD
+    phases = 2 * kv_heads
 
     def own_load(ph):
-        return pltpu.make_async_copy(weights[ph], wbuf.at[ph, me], own_sem.at[ph])
+        ref, h = (wv_ref, ph) if ph < kv_heads else (wk_ref, ph - kv_heads)
+        return pltpu.make_async_copy(
+            ref.at[:, h * HD : (h + 1) * HD], wbuf.at[ph, me], own_sem.at[ph]
+        )
 
     def start_own(ph):
         both_ways(lambda up: main_copy(ph, z, up).start())
@@ -208,8 +214,8 @@
         xtail_copy(ph, peer_x).wait_recv()
         both_ways(lambda up: tail_copy(ph, z, up).start())
 
-    own_load(0).start()
-    own_load(1).start()
+    for ph in range(phases):
+        own_load(ph).start()
     tok_load = pltpu.make_async_copy(tok_ref, tok, tok_sem)
     tok_load.start()
     cache_load = pltpu.make_async_copy(cache_ref, cache, cache_sem)
@@ -225,10 +231,11 @@
         )
     pl.semaphore_wait(barrier, n_group - 1)
 
-    own_load(0).wait()
-    start_own(0)
+    for ph in range(phases):
+        own_load(ph).wait()
+        if ph < 2:
+            start_own(ph)
     acc[...] = jnp.zeros_like(acc)
-    own_load(1).wait()
     tok_load.wait()
 
     chunk = 32
@@ -296,7 +303,6 @@
 
     query_f[...] = query_ref[...].astype(jnp.float32)
     heads = query_f.shape[1] // HD
-    kv_heads = cols // HD
     share = heads // kv_heads
     group_rows = heads * CAP
     span_rows = cache.shape[0] // n_group
@@ -336,46 +342,45 @@
         near_max[rows, :] = jnp.broadcast_to(top, (group_rows, HD))
         near_sum[rows, :] = jnp.broadcast_to(total, (group_rows, HD))
 
-    def fresh(i):
-        rows = slice(i * group_rows, (i + 1) * group_rows)
-        each = group_rows // kv_heads
-        found = []
-        for h in range(kv_heads):
-            asked = query_b[i * group_rows + h * each : i * group_rows + (h + 1) * each, :]
-            found.append(
-                lax.dot_general(
-                    asked,
-                    rbuf[1, i, :, h * HD : (h + 1) * HD],
-                    (((1,), (1,)), ((), ())),
-                    preferred_element_type=jnp.float32,
-                )
-            )
-        scores = jnp.concatenate(found, 0)
+    each = group_rows // kv_heads
+
+    def fresh(i, h):
+        rows = slice(i * group_rows + h * each, i * group_rows + (h + 1) * each)
+        scores = lax.dot_general(
+            query_b[rows, :],
+            rbuf[kv_heads + h, i],
+            (((1,), (1,)), ((), ())),
+            preferred_element_type=jnp.float32,
+        )
         page = grid_of((1, every), 1) // owned_pages
         sent = (owner_row == me.astype(jnp.float32)) & (page == i)
         number = jnp.sum(jnp.where(sent, 1.0, 0.0), 1, keepdims=True)
         slot = grid_of((1, CAP * PAGE), 1) // PAGE
-        ok = (slot == row_slot) & (slot.astype(jnp.float32) < number)
+        ok = (slot == grid_of((each, 1), 0) % CAP) & (slot.astype(jnp.float32) < number)
         scores = jnp.where(ok, scores * scale, -1e30)
         old_top = near_max[rows, :]
         top = jnp.maximum(jnp.max(scores, 1, keepdims=True), old_top)
         weights = jnp.where(ok, jnp.exp(scores - top), 0.0)
         keep = jnp.exp(old_top - top)
         total = near_sum[rows, :] * keep + jnp.sum(weights, 1, keepdims=True)
-        weights = weights.astype(jnp.bfloat16)
-        mixed = [
-            jnp.dot(
-                weights[h * each : (h + 1) * each, :],
-                rbuf[0, i, :, h * HD : (h + 1) * HD],
-                preferred_element_type=jnp.float32,
-            )
-            for h in range(kv_heads)
-        ]
-        final = (near_out[rows, :] * keep + jnp.concatenate(mixed, 0)) / total
-        for j in range(heads):
-            result[i * CAP : (i + 1) * CAP, j * HD : (j + 1) * HD] = final[
+        mixed = jnp.dot(
+            weights.astype(jnp.bfloat16), rbuf[h, i], preferred_element_type=jnp.float32
+        )
+        final = (near_out[rows, :] * keep + mixed) / total
+        for j in range(share):
+            at_col = (h * share + j) * HD
+            result[i * CAP : (i + 1) * CAP, at_col : at_col + HD] = final[
                 j * CAP : (j + 1) * CAP, :
             ]
+
+    def finish(h):
+        for ph in (h, kv_heads + h):
+            for step in range(1, n_group):
+                page_wait(ph, step)
+        for i in range(n_group):
+            fresh(i, h)
+        span = slice(h * share * HD, (h + 1) * share * HD)
+        out_ref[:, span] = result[:, span].astype(jnp.bfloat16)
 
     half = count // 2
 
@@ -409,13 +414,8 @@
 
     def hand_over(ph):
         held = acc[ph]
-        if ph == 1:
-            turned = [
-                held[:, s : s + HD] * cos_ref[...]
-                + pltpu.roll(held[:, s : s + HD], HD // 2, 1) * sin_ref[...]
-                for s in range(0, cols, HD)
-            ]
-            held = jnp.concatenate(turned, -1)
+        if ph >= kv_heads:
+            held = held * cos_ref[...] + pltpu.roll(held, HD // 2, 1) * sin_ref[...]
         held = held.astype(jnp.bfloat16)
 
         for owner in range(n_group):
@@ -442,9 +442,9 @@
         def _():
             copy(ph, zz, False).start()
 
-    @pl.loop(0, 2 * line + 1)
+    @pl.loop(0, phases * line + PEER_LAG)
     def _(step):
-        @pl.when(step < 2 * line)
+        @pl.when(step < phases * line)
         def _():
             @pl.loop(0, 2)
             def _(way):
@@ -456,57 +456,61 @@
                     forward(ph, dist, zz, way, main_copy)
                     xhead_copy(ph, zz, x).start()
 
+            following = lax.div(step, line) + 1
+
+            @pl.when((lax.rem(step, line) == 1) & (following + 1 < phases))
+            def _():
+                start_own(following + 1)
+
+            @pl.when((lax.rem(step, line) == 2) & (following < phases))
+            def _():
+                pass_own_tail(following)
+
             @pl.loop(0, 2)
             def _(way):
                 ph, dist, zz, live = at(step, way)
+
+                @pl.when(live)
+                def _():
+                    multiply(ph, zz * 2 + x)
+
+            @pl.when(step < n_group)
+            def _():
+                near(step)
+
+        @pl.when((step >= TAIL_LAG) & (step < phases * line + TAIL_LAG))
+        def _():
+            @pl.loop(0, 2)
+            def _(way):
+                ph, dist, zz, live = at(step - TAIL_LAG, way)
 
                 @pl.when(live & (dist > 0))
                 def _():
                     tail_copy(ph, zz, True).wait_recv()
                     forward(ph, dist, zz, way, tail_copy)
 
-            @pl.when(step == 1)
-            def _():
-                start_own(1)
-
-            @pl.when(step == 2)
-            def _():
-                pass_own_tail(1)
-
-            @pl.loop(0, 2)
-            def _(way):
-                ph, dist, zz, live = at(step, way)
-
-                @pl.when(live)
-                def _():
-                    multiply(ph, zz * 2 + x)
-
-            near(step)
-
-        @pl.when(step > 0)
+        @pl.when(step >= PEER_LAG)
         def _():
             @pl.loop(0, 2)
             def _(way):
-                ph, dist, zz, live = at(step - 1, way)
+                ph, dist, zz, live = at(step - PEER_LAG, way)
 
                 @pl.when(live)
                 def _():
                     xhead_copy(ph, zz, peer_x).wait_recv()
                     multiply(ph, zz * 2 + peer_x)
 
-        @pl.when(step == line)
-        def _():
-            hand_over(0)
-
-    hand_over(1)
-    for ph in range(2):
-        for step in range(1, n_group):
-            page_wait(ph, step)
-    for i in range(n_group):
-        fresh(i)
-    out_ref[...] = result[...].astype(jnp.bfloat16)
-
-    for ph in range(2):
+        for ph in range(phases - 1):
+
+            @pl.when(step == (ph + 1) * line + PEER_LAG - 1)
+            def _():
+                hand_over(ph)
+
+    hand_over(phases - 1)
+    for h in range(kv_heads):
+        finish(h)
+
+    for ph in range(phases):
         xtail_copy(ph, x).wait_send()
         for zz in range(line):
             xhead_copy(ph, zz, x).wait_send()
@@ -534,6 +538,7 @@
     line = n_group // 2
     slots = n_group * CAP * PAGE
     cut = depth - depth // 8
+    phases = 2 * cols // HD
     rows = queries.shape[0]
     asked = rows * queries.shape[1] // HD
     cache = kv_cache.reshape(-1, HD)
@@ -548,11 +553,11 @@
         out_specs=vmem,
         scratch_shapes=[
             pltpu.VMEM((count, width), bf16),
-            pltpu.VMEM((2, n_group, depth, cols), bf16),
-            pltpu.VMEM((2, count, cols), f32),
+            pltpu.VMEM((phases, n_group, depth, HD), bf16),
+            pltpu.VMEM((phases, count, HD), f32),
             pltpu.VMEM((slots, count), bf16),
-            pltpu.VMEM((2, n_group, slots // n_group, cols), bf16),
-            pltpu.VMEM((2, n_group, slots // n_group, cols), bf16),
+            pltpu.VMEM((phases, n_group, slots // n_group, HD), bf16),
+            pltpu.VMEM((phases, n_group, slots // n_group, HD), bf16),
             pltpu.VMEM((count, HD), f32),
             pltpu.VMEM((count, HD), f32),
             pltpu.VMEM(cache.shape, bf16),
@@ -564,18 +569,18 @@
             pltpu.VMEM(queries.shape, f32),
             dma,
             dma,
-            dma((2,)),
-            dma((2, line)),
-            dma((2, line)),
-            dma((2, line)),
-            dma((2, line)),
-            dma((2, line)),
-            dma((2, line)),
-            dma((2, line)),
-            dma((2,)),
-            dma((2, line)),
-            dma((2, n_group)),
-            dma((2, n_group)),
+            dma((phases,)),
+            dma((phases, line)),
+            dma((phases, line)),
+            dma((phases, line)),
+            dma((phases, line)),
+            dma((phases, line)),
+            dma((phases, line)),
+            dma((phases, line)),
+            dma((phases,)),
+            dma((phases, line)),
+            dma((phases, n_group)),
+            dma((phases, n_group)),
         ],
         compiler_params=pltpu.CompilerParams(
             collective_id=0, has_side_effects=True, vmem_limit_bytes=VMEM_BUDGET
@@ -608,7 +613,7 @@
 def pick(tokens, norm_gain, w_key, *rest):
     ngroup = lax.axis_size("group")
     count, width = tokens.shape
-    fused = ngroup % 2 == 0 and count % 256 == 0 and w_key.shape[0] % 1024 == 0
+    fused = ngroup >= 6 and ngroup % 2 == 0 and count % 256 == 0 and w_key.shape[0] % 1024 == 0
     fused = fused and fits(count, width, w_key.shape[1], ngroup)
     return (per_device_fused if fused else per_device)(tokens, norm_gain, w_key, *rest)
 

time: 122 us -> 116 us (0.951)
  Pallas kernels: 120 us -> 114 us
    pallas_call x1, Pallas kernels: 120 us -> 114 us  [per_device_fused(): pl.pallas_call(functools.partial(project_kernel, n_group, cut), out_shape...]
where the time goes in v3:
time: 116 us; the launch traced here: 115 us
  Pallas kernels  114 us (98%)
  local copies, waits for them, and re-layouts  1.67 us (1%)
    pallas_call x1, Pallas kernels, per_device_fused(): pl.pallas_call(functools.partial(project_kernel, n_group, cut), out_shape...  114 us

profile of v3, /device:TPU:0, one launch (start us, length us, event | category | flops | bytes accessed | tf_op | source)
XLA Modules:
  0.0 115.4 jit_solution(15937423531576708951)
XLA Ops:
  0.0 113.7 %shard_map.91 = bf16[64,2048]{1,0:T(8,128)(2,1)} custom-call(bf16[512,8192]{1,0:T(8,128)(2,1)} %tok_ref.1, f32[1,8192]{1,0:T(1,128)} %bitcast.6, bf16[1024,256]{1,0:T(8,128)(2,1)} %wk_ref.1, bf16[1024,256]{1,0:T(8,128)(2,1)} %wv_ref.1, s32[1,512]{1,0:T(1,128)} %bitcast.7, s32[1,256]{1,0:T(1,128)} %bitcast.8, bf16[64,2048]{1,0:T(8,128)(2,1)} %query_ref.1, ...), custom_call_target="tpu_custom_call" | custom-call | flops 4294967296 | bytes 9437184 | tf_op jit(solution)/shard_map/pallas_call | solution.py:549
  113.8 1.7 %copy.11 = bf16[64,2048]{1,0:T(8,128)(2,1)} copy(bf16[64,2048]{1,0:T(8,128)(2,1)} %shard_map.91) | data formatting | bytes 524288

commit v4 on v3

--- a/solution.py
+++ b/solution.py
@@ -537,7 +537,7 @@
     n_group = lax.axis_size("group")
     line = n_group // 2
     slots = n_group * CAP * PAGE
-    cut = depth - depth // 8
+    cut = depth - depth * 3 // 32
     phases = 2 * cols // HD
     rows = queries.shape[0]
     asked = rows * queries.shape[1] // HD

time: 116 us -> 117 us (level)
    pallas_call x1, Pallas kernels: 114 us -> 115 us  [per_device_fused(): pl.pallas_call(functools.partial(project_kernel, n_group, cut), out_shape...]
where the time goes in v4:
time: 117 us
  Pallas kernels  115 us (98%)
  local copies, waits for them, and re-layouts  1.67 us (1%)
    pallas_call x1, Pallas kernels, per_device_fused(): pl.pallas_call(functools.partial(project_kernel, n_group, cut), out_shape...  115 us

profile of v4, /device:TPU:0, one launch (start us, length us, event | category | flops | bytes accessed | tf_op | source)
XLA Modules:
  0.0 116.7 jit_solution(12911079305072565194)
XLA Ops:
  0.0 115.0 %shard_map.91 = bf16[64,2048]{1,0:T(8,128)(2,1)} custom-call(bf16[512,8192]{1,0:T(8,128)(2,1)} %tok_ref.1, f32[1,8192]{1,0:T(1,128)} %bitcast.6, bf16[1024,256]{1,0:T(8,128)(2,1)} %wk_ref.1, bf16[1024,256]{1,0:T(8,128)(2,1)} %wv_ref.1, s32[1,512]{1,0:T(1,128)} %bitcast.7, s32[1,256]{1,0:T(1,128)} %bitcast.8, bf16[64,2048]{1,0:T(8,128)(2,1)} %query_ref.1, ...), custom_call_target="tpu_custom_call" | custom-call | flops 4294967296 | bytes 9437184 | tf_op jit(solution)/shard_map/pallas_call | solution.py:549
  115.0 1.7 %copy.11 = bf16[64,2048]{1,0:T(8,128)(2,1)} copy(bf16[64,2048]{1,0:T(8,128)(2,1)} %shard_map.91) | data formatting | bytes 524288
